TPU v7x, 32 devices: a whole 2x2x4 slice. The times are simulated.
32 devices in a mesh: dp: 8 (over z, x), mp: 4 (over y, core).
Axes of the slice: x: 2, y: 2, z: 4, core: 2. Of those that a mesh axis runs over, the one named last changes fastest.
Arguments:
- tokens: bfloat16 [32768, 768], P(('dp', 'mp')), may hold values from -6 to 6
- segments: int32 [64, 512], P(('dp', 'mp')), may hold values from 0 to 5, never falling along the last dimension, each value on 1 to 256 neighbouring positions
- head_mask: int32 [12], replicated, may hold values 0 or 1
- unit_mask: int32 [3072], replicated, may hold values 0 or 1
- hidden_mask: int32 [768], replicated, may hold values 0 or 1
- layer_gates: float32 [2], replicated, may hold values from 0.5 to 1.5
- qkv_weight: bfloat16 [768, 2304], P('mp'), may hold values from -0.21875 to 0.21875
- out_weight: bfloat16 [768, 768], P('mp'), may hold values from -1.75 to 1.75
- norm_gain: float32 [768], replicated, may hold values from 0.5 to 1.5
- norm_bias: float32 [768], replicated, may hold values from -3 to 3
- up_weight: bfloat16 [768, 3072], P(None, 'mp'), may hold values from -0.21875 to 0.21875
- down_weight: bfloat16 [768, 3072], P(None, 'mp'), may hold values from -0.109375 to 0.109375
- cotangent: bfloat16 [32768, 768], P(('dp', 'mp')), may hold values from -6 to 6
- owner_slot: int32 [48], replicated, may hold values from 0 to 47, as said below
- master: float32 [48, 384, 384], P('dp', 'mp'), may hold values from -0.21875 to 0.21875
- left_stats: float32 [48, 384, 384], P('dp', 'mp'), may hold values from -12582912 to 50331648
- right_stats: float32 [48, 384, 384], P('dp', 'mp'), may hold values from -12582912 to 50331648
- left_root: float32 [48, 384, 384], P('dp', 'mp'), may hold values from -1 to 1
- right_root: float32 [48, 384, 384], P('dp'), may hold values from -1 to 1
Outputs:
- output: bfloat16 [32768, 768], P(('dp', 'mp'))
- input_grad: float32 [32768, 768], P(('dp', 'mp'))
- head_grad: float32 [12], replicated
- unit_grad: float32 [3072], replicated
- hidden_grad: float32 [768], replicated
- layer_grad: float32 [2], replicated
- norm_grad: float32 [2, 768], replicated
- norm_new: float32 [2, 768], replicated
- block_grad: float32 [48, 384, 384], P('dp', 'mp')
- left_new: float32 [48, 384, 384], P('dp', 'mp')
- right_new: float32 [48, 384, 384], P('dp', 'mp')
- weight_new: float32 [48, 384, 384], P('dp', 'mp')
- weight_copy: bfloat16 [48, 384, 384], P('dp', 'mp')
Inputs may be any that keep to these rules, and one draw needn't show every extreme that they name: `segments`: in every block of 512 positions the item numbers run from 0 to 5 and never fall; each item has 1 to 256 positions, and one item of each block has exactly 256. `owner_slot`: every slot number appears exactly once.
All inputs are finite; a program needn't handle non-finite values.
Results may differ from a plain program's by a relative error of at most 0.017.
Values may be sent and summed in bfloat16 or wider, within the bound.
A program may use at most 192 MiB of HBM per device.

v0:
```python
from functools import partial
import math

import jax
import jax.numpy as jnp
from jax import lax
from jax.experimental import pallas as pl
from jax.experimental.pallas import tpu as pltpu
from jax.sharding import PartitionSpec as P

FF = 3072
SB = 384


HIGH = lax.Precision.HIGHEST
BETA = 0.5
RATE = 0.5
EPS = 1e-12
MASKED = -1e30


def gelu_exact(values):
    return jax.nn.gelu(values, approximate=False)


def normalize(summed, gain_in, offset, hidden_gate):
    centre = summed - jnp.mean(summed, axis=-1, keepdims=True)
    spread = jnp.mean(centre * centre, axis=-1, keepdims=True)
    return (centre * lax.rsqrt(spread + EPS) * gain_in + offset) * hidden_gate


def split_heads(block_joined, head_count):
    pieces = block_joined.reshape(block_joined.shape[0], 3, head_count, -1)
    return (pieces[:, 0], pieces[:, 1], pieces[:, 2])


def masked_scores(queries, keys_in, labels, factor):
    scores = (
        jnp.einsum("qhd,khd->hqk", queries, keys_in, preferred_element_type=jnp.float32) * factor
    )
    allowed = labels[:, None] == labels[None, :]
    return jnp.where(allowed[None], scores, MASKED)


def attend_forward(packed, head_count, factor):
    block_joined, labels = packed
    queries, keys_in, values_in = split_heads(block_joined, head_count)
    scores = masked_scores(queries, keys_in, labels, factor)
    highest = jnp.max(scores, axis=-1, keepdims=True)
    raised = jnp.exp(scores - highest)
    totals = jnp.sum(raised, axis=-1, keepdims=True)
    weights_low = (raised / totals).astype(jnp.bfloat16)
    context = jnp.einsum("hqk,khd->qhd", weights_low, values_in, preferred_element_type=jnp.float32)
    return (context, (highest + jnp.log(totals))[:, :, 0])


def attend_backward(packed, head_count, factor):
    block_joined, log_totals, context_grad, labels = packed
    queries, keys_in, values_in = split_heads(block_joined, head_count)
    scores = masked_scores(queries, keys_in, labels, factor)
    weights_full = jnp.exp(scores - log_totals[:, :, None])
    weights_low = weights_full.astype(jnp.bfloat16)
    values_grad = jnp.einsum(
        "hqk,qhd->khd", weights_low, context_grad, preferred_element_type=jnp.float32
    )
    weights_grad = jnp.einsum(
        "qhd,khd->hqk", context_grad, values_in, preferred_element_type=jnp.float32
    )
    inner_sum = jnp.sum(weights_full * weights_grad, axis=-1, keepdims=True)
    scores_grad = (weights_full * (weights_grad - inner_sum)).astype(jnp.bfloat16)
    queries_grad = (
        jnp.einsum("hqk,khd->qhd", scores_grad, keys_in, preferred_element_type=jnp.float32)
        * factor
    )
    keys_grad = (
        jnp.einsum("hqk,qhd->khd", scores_grad, queries, preferred_element_type=jnp.float32)
        * factor
    )
    merged = jnp.concatenate([queries_grad, keys_grad, values_grad], axis=1)
    return merged.reshape(merged.shape[0], -1).astype(jnp.bfloat16)


def contract_rows(left, right):
    return lax.dot_general(
        left, right, (((0,), (0,)), ((), ())), preferred_element_type=jnp.float32
    )


def contract_cols(left, right):
    return lax.dot_general(
        left, right, (((1,), (1,)), ((), ())), preferred_element_type=jnp.float32
    )


def body(
    tokens,
    segments,
    head_mask,
    unit_mask,
    hidden_mask,
    layer_gates,
    qkv_weight,
    out_weight,
    norm_gain,
    norm_bias,
    up_weight,
    down_weight,
    cotangent,
    owner_slot,
    master,
    left_stats,
    right_stats,
    left_root,
    right_root,
):
    row_count = tokens.shape[0]
    width = tokens.shape[1]
    head_count = head_mask.shape[0]
    head_width = width // head_count
    block_rows = segments.shape[1]
    block_count = segments.shape[0]
    factor = 1.0 / math.sqrt(head_width)
    model_size = lax.axis_size("mp")
    share = FF // model_size
    part_rows = SB // model_size
    total_tokens = row_count * lax.axis_size("dp") * model_size
    head_gate = head_mask.astype(jnp.float32)
    unit_gate = unit_mask.astype(jnp.float32)
    hidden_gate = hidden_mask.astype(jnp.float32)
    inputs = tokens.astype(jnp.float32)
    back_full = cotangent.astype(jnp.float32)
    qkv_full, out_full, up_full, down_full = (
        lax.all_gather(qkv_weight, "mp", axis=0, tiled=True),
        lax.all_gather(out_weight, "mp", axis=0, tiled=True),
        lax.all_gather(up_weight, "mp", axis=1, tiled=True),
        lax.all_gather(down_weight, "mp", axis=1, tiled=True),
    )
    joined_qkv = jnp.dot(tokens, qkv_full, preferred_element_type=jnp.float32).astype(jnp.bfloat16)
    joined_blocks = joined_qkv.reshape(block_count, block_rows, 3 * width)
    context, log_totals = lax.map(
        partial(attend_forward, head_count=head_count, factor=factor), (joined_blocks, segments)
    )
    context = context.reshape(row_count, head_count, head_width)
    gated_low = (context * head_gate[None, :, None]).reshape(row_count, width).astype(jnp.bfloat16)
    attn_out = jnp.dot(gated_low, out_full, preferred_element_type=jnp.float32)
    summed = inputs + layer_gates[0] * attn_out
    hidden, norm_pull = jax.vjp(normalize, summed, norm_gain, norm_bias, hidden_gate)
    hidden_low = hidden.astype(jnp.bfloat16)
    pre_act = jnp.dot(hidden_low, up_full, preferred_element_type=jnp.float32)
    active, gelu_pull = jax.vjp(gelu_exact, pre_act)
    active_low = (active * unit_gate).astype(jnp.bfloat16)
    branch = contract_cols(active_low, down_full)
    output = (hidden + layer_gates[1] * branch).astype(jnp.bfloat16)
    back_rounded = (layer_gates[1] * back_full).astype(jnp.bfloat16)
    qkv_full, out_full, up_full, down_full = (
        lax.all_gather(qkv_weight, "mp", axis=0, tiled=True),
        lax.all_gather(out_weight, "mp", axis=0, tiled=True),
        lax.all_gather(up_weight, "mp", axis=1, tiled=True),
        lax.all_gather(down_weight, "mp", axis=1, tiled=True),
    )
    grad_active = jnp.dot(back_rounded, down_full, preferred_element_type=jnp.float32)
    unit_grad = jnp.sum(grad_active * active, axis=0)
    grad_inner = gelu_pull(grad_active * unit_gate)[0].astype(jnp.bfloat16)
    hidden_back = contract_cols(grad_inner, up_full)
    up_term = contract_rows(grad_inner, hidden_low)
    down_term = contract_rows(active_low, back_rounded)
    unit_local = (
        lax.psum_scatter(
            jnp.stack([up_term, down_term], axis=1).astype(jnp.bfloat16),
            "mp",
            scatter_dimension=0,
            tiled=True,
        )
        .astype(jnp.float32)
        .transpose(1, 2, 0)
    )
    summed_grad, gain_grad, bias_grad, mask_grad = norm_pull(back_full + hidden_back)
    layer_grad = jnp.stack([jnp.sum(summed_grad * attn_out), jnp.sum(back_full * branch)])
    out_back = (layer_gates[0] * summed_grad).astype(jnp.bfloat16)
    gated_grad = contract_cols(out_back, out_full).astype(jnp.bfloat16)
    gated_heads = gated_grad.reshape(row_count, head_count, head_width)
    head_grad = jnp.sum(context * gated_heads.astype(jnp.float32), axis=(0, 2))
    context_grad = gated_heads * head_mask.astype(jnp.bfloat16)[None, :, None]
    joined_grad = lax.map(
        partial(attend_backward, head_count=head_count, factor=factor),
        (
            joined_blocks,
            log_totals,
            context_grad.reshape(block_count, block_rows, head_count, head_width),
            segments,
        ),
    )
    joined_grad = joined_grad.reshape(row_count, 3 * width)
    input_grad = summed_grad + contract_cols(joined_grad, qkv_full)
    tiles = width // SB
    qkv_term = jnp.einsum(
        "tri,tcj->rcij",
        tokens.reshape(row_count, tiles, SB),
        joined_grad.reshape(row_count, 3 * tiles, SB),
        preferred_element_type=jnp.float32,
    )
    out_term = jnp.einsum(
        "tri,tcj->rcij",
        gated_low.reshape(row_count, tiles, SB),
        out_back.reshape(row_count, tiles, SB),
        preferred_element_type=jnp.float32,
    )
    attn_terms = jnp.concatenate(
        [
            qkv_term.reshape(-1, model_size, part_rows, SB),
            out_term.reshape(-1, model_size, part_rows, SB),
        ],
        axis=0,
    )
    attn_rows = (
        lax.psum_scatter(attn_terms.astype(jnp.bfloat16), "mp", scatter_dimension=1, tiled=True)
        .astype(jnp.float32)
        .reshape(-1, part_rows, SB)
    )
    unit_split = unit_local.reshape(2, tiles, model_size, part_rows, share)
    unit_rows = lax.all_to_all(
        unit_split.astype(jnp.bfloat16), "mp", split_axis=2, concat_axis=4, tiled=True
    ).astype(unit_split.dtype)
    unit_rows = (
        unit_rows.reshape(2, tiles, part_rows, FF // SB, SB)
        .transpose(0, 1, 3, 2, 4)
        .reshape(-1, part_rows, SB)
    )
    all_rows = jnp.concatenate([attn_rows, unit_rows], axis=0)
    slot_count = owner_slot.shape[0]
    pick = (owner_slot[None, :] == jnp.arange(slot_count)[:, None]).astype(jnp.bfloat16)
    flat_rows = all_rows.astype(jnp.bfloat16).reshape(slot_count, -1)
    slotted = jnp.dot(pick, flat_rows, preferred_element_type=jnp.float32).reshape(all_rows.shape)
    owned = lax.psum_scatter(
        slotted.astype(jnp.bfloat16), "dp", scatter_dimension=0, tiled=True
    ).astype(jnp.float32)
    full_grad = lax.all_gather(owned.astype(jnp.bfloat16), "mp", axis=1, tiled=True).astype(
        owned.dtype
    )
    row_start = lax.axis_index("mp") * part_rows
    columns = lax.dynamic_slice_in_dim(full_grad, row_start, part_rows, 2)
    left_new = BETA * left_stats + (1.0 - BETA) * jnp.einsum(
        "srj,skj->srk", owned, full_grad, precision=HIGH
    )
    right_new = BETA * right_stats + (1.0 - BETA) * jnp.einsum(
        "sjr,sjk->srk", columns, full_grad, precision=HIGH
    )
    left_part = jnp.einsum("sri,sij->srj", left_root, full_grad, precision=HIGH)
    update = jnp.einsum("srj,sjk->srk", left_part, right_root, precision=HIGH)
    weight_new = master - RATE * update
    norm_grad = jnp.stack([gain_grad, bias_grad])
    norm_grad, mask_grad, head_grad, layer_grad, unit_grad = lax.psum(
        (norm_grad, mask_grad, head_grad, layer_grad, unit_grad), ("dp", "mp")
    )
    norm_new = jnp.stack([norm_gain, norm_bias]) - 0.2 / math.sqrt(total_tokens) * norm_grad
    return (
        output,
        input_grad,
        head_grad,
        unit_grad,
        mask_grad,
        layer_grad,
        norm_grad,
        norm_new,
        owned,
        left_new,
        right_new,
        weight_new,
        weight_new.astype(jnp.bfloat16),
    )


F32 = jnp.float32
BF = jnp.bfloat16
MESH = pl.DeviceIdType.MESH
LOG2E = 1.4426950408889634
ROWS = 1024
D = 768
HD = 64
BLK = 512
NT_DIMS = (((1,), (1,)), ((), ()))
NN_DIMS = (((1,), (0,)), ((), ()))


def nn(left, right):
    return lax.dot_general(left, right, NN_DIMS, preferred_element_type=F32)


def nt(left, right):
    return lax.dot_general(left, right, NT_DIMS, preferred_element_type=F32)


def coords():
    d = lax.axis_index("dp")
    m = lax.axis_index("mp")
    return d // 2, d % 2, m // 2, m % 2


def at(z, x, y, c):
    return (2 * z + x, 2 * y + c)


def gelu_parts(x):
    ax = jnp.abs(x)
    e = jnp.exp2(x * x * (-0.5 * LOG2E))
    t = 1.0 / (1.0 + (0.3275911 * math.sqrt(0.5)) * ax)
    poly = t * (
        0.5 * 0.254829592
        + t
        * (
            -0.5 * 0.284496736
            + t * (0.5 * 1.421413741 + t * (-0.5 * 1.453152027 + t * (0.5 * 1.061405429)))
        )
    )
    tail = poly * e
    cdf = jnp.where(x < 0, tail, 1.0 - tail)
    active = x * cdf
    return active, cdf + x * (e * (1.0 / math.sqrt(2.0 * math.pi)))


def colsum(v):
    return jnp.sum(v, axis=0, keepdims=True)


def row_norm(summed):
    centre = summed - jnp.mean(summed, axis=-1, keepdims=True)
    spread = jnp.mean(centre * centre, axis=-1, keepdims=True)
    inv = lax.rsqrt(spread + EPS)
    return centre * inv, inv


def one_row(v):
    return jnp.concatenate([v[i : i + 1] for i in range(v.shape[0])], axis=1)


def many_rows(v):
    return jnp.concatenate([v[:, 128 * i : 128 * i + 128] for i in range(v.shape[1] // 128)], axis=0)


def head_lanes(heads):
    which = lax.broadcasted_iota(jnp.int32, (1, D), 1) // HD
    row = jnp.zeros((1, D), F32)
    for h in range(12):
        row = row + jnp.where(which == h, heads[h].astype(F32), 0.0)
    return row


HALF = BLK // 2


def first_rows(segs):
    values = segs[...].astype(F32)
    begin = jnp.zeros((2, 1), F32)
    for item in range(6):
        count = jnp.sum(jnp.where(values == item, 1.0, 0.0), axis=1, keepdims=True)
        before = jnp.sum(jnp.where(values < item, 1.0, 0.0), axis=1, keepdims=True)
        begin = begin + jnp.where(count == HALF, before, 0.0)
    return begin


def turning(begin, sign):
    row = lax.broadcasted_iota(jnp.int32, (BLK, BLK), 0).astype(F32)
    col = lax.broadcasted_iota(jnp.int32, (BLK, BLK), 1).astype(F32)
    off = sign * (col - row) - begin
    return jnp.where((off == 0) | (off == -BLK), 1.0, 0.0)


def turn_labels(segs, begin, segcol, segrow):
    for b in range(2):
        hot = turning(begin[b : b + 1], 1)[HALF:, :]
        column = jnp.sum(hot * segs[b : b + 1, :].astype(F32), axis=1, keepdims=True)
        segcol[b] = column
        segrow[b] = jnp.broadcast_to(column, (HALF, 128)).T[0:1, :]


MOVED = (8, 8, 4)
LEFT = 8 - MOVED[2]
NPIECE = 8


def forward_kernel(
    gates,
    heads,
    tokens_in,
    cot_in,
    segs,
    units,
    hidden,
    gain_in,
    bias_in,
    qkv_in,
    out_in,
    up_in,
    down_in,
    o_out,
    o_joined,
    o_ctx,
    o_ctxT,
    o_tokT,
    o_sgrad,
    o_sums,
    o_far,
    o_wq,
    o_wo,
    lse,
    small,
    wq,
    wo,
    wu,
    wd,
    joined,
    ctx,
    ctxT,
    tokT,
    attn,
    blow,
    bT,
    branch,
    hback,
    grads,
    got1,
    got2,
    tokens,
    cot,
    segcol,
    segrow,
    ugate,
    vec,
    send_sem,
    recv_sem,
    loc_sem,
    out_sem,
    c_send,
    c_recv,
    x_send,
    x_recv,
):
    z, x, y, c = coords()
    hT = tokT
    hlow = ctx
    act, inner, outv = (joined.at[:, pl.ds(D * i, D)] for i in range(3))
    m = 2 * y + c
    ms = 2 * y + 1 - c
    my = 2 * (1 - y) + c
    mys = 2 * (1 - y) + 1 - c
    sib = at(z, x, y, 1 - c)
    ypeer = at(z, x, 1 - y, c)
    xpeer = at(z, 1 - x, y, c)
    zpeer = at(z + 1 - 2 * (z % 2), x, y, c)
    g0 = gates[0]
    g1 = gates[1]

    barrier = pltpu.get_barrier_semaphore()
    for peer in (sib, ypeer, xpeer, zpeer):
        pl.semaphore_signal(barrier, inc=1, device_id=peer, device_id_type=MESH)
    loads = (
        pltpu.make_async_copy(tokens_in, blow, out_sem.at[6]),
        pltpu.make_async_copy(cot_in, ctx, out_sem.at[7]),
    )
    for copy in loads:
        copy.start()
    begin = first_rows(segs)
    pl.semaphore_wait(barrier, 4)

    def spot(j):
        if j < 3:
            return 0, 192, pl.ds(768 * j, 768)
        if j == 3:
            return 1, 192, slice(None)
        return 2 + (j - 4) // 2, 768, pl.ds(384 * (j % 2), 384)

    def full(j, i, h=None):
        which, n, cols = spot(j)
        ref = (wq, wo, wu, wd)[which]
        if h is None:
            return ref.at[i, :, cols]
        return ref.at[i, pl.ds(pl.multiple_of(h * (n // 2), 16), n // 2), cols]

    def own(j, h=None):
        which, n, cols = spot(j)
        ref = (qkv_in, out_in, up_in, down_in)[which]
        if h is None:
            return ref.at[:, cols]
        return ref.at[pl.ds(pl.multiple_of(h * (n // 2), 16), n // 2), cols]

    def remote(src, dst, j, k, dev):
        return pltpu.make_async_remote_copy(
            src_ref=src,
            dst_ref=dst,
            send_sem=send_sem.at[j, k],
            recv_sem=recv_sem.at[j, k],
            device_id=dev,
            device_id_type=MESH,
        )

    def s1(j):
        return remote(own(j), full(j, m), j, 0, sib)

    def half_of(j):
        return (x, xpeer) if j < 4 else (z % 2, zpeer)

    def s2(j):
        h, _ = half_of(j)
        return remote(own(j, h), full(j, m, h), j, 1, ypeer)

    def s3(j):
        h, peer = half_of(j)
        return remote(full(j, my, h), full(j, my, h), j, 2, peer)

    def s4(j):
        h, _ = half_of(j)
        return remote(full(j, my, h), full(j, my, h), j, 3, sib)

    def s5(j):
        h, _ = half_of(j)
        return remote(full(j, my, 1 - h), full(j, my, 1 - h), j, 4, sib)

    def local(j):
        return pltpu.make_async_copy(own(j), full(j, m), loc_sem.at[j])

    def first(j):
        s2(j).start()
        s1(j).start()
        local(j).start()

    def second(j):
        s2(j).wait_recv()
        s3(j).start()
        s4(j).start()

    def third(j):
        s3(j).wait_recv()
        s5(j).start()

    def finish_near(j):
        local(j).wait()
        s1(j).wait_recv()

    def finish_far(j):
        s4(j).wait_recv()
        s5(j).wait_recv()

    def finish_sends(j):
        for s in (s1, s2, s3, s4, s5):
            s(j).wait_send()

    for j in range(3):
        first(j)

    turn_labels(segs, begin, segcol, segrow)
    for copy in loads:
        copy.wait()
    def turn(src, dst):
        @pl.loop(0, 2)
        def _(b):
            hot = turning(jnp.where(b == 0, begin[0:1], begin[1:2]), 1).astype(BF)
            rows = pl.ds(pl.multiple_of(b * BLK, BLK), BLK)
            dst[rows, :] = nn(hot, src[rows, :]).astype(BF)

    def backs(lo, hi):
        @pl.loop(lo, hi)
        def _(r):
            rows = pl.ds(pl.multiple_of(r * 256, 256), 256)
            low = (g1 * cot[rows, :].astype(F32)).astype(BF)
            blow[rows, :] = low
            bT[:, rows] = low.T

    turn(blow, tokens)

    near_sum = (attn, branch, hback)

    def project(j, near):
        yy = y if near else 1 - y

        @pl.loop(0, 2)
        def _(r):
            rows = pl.ds(pl.multiple_of(r * 512, 512), 512)
            w = wq[pl.ds(2 * yy, 2), :, pl.ds(768 * j, 768)].reshape(SB, D)
            one = nn(tokens[rows, pl.ds(pl.multiple_of(SB * yy, 128), SB)], w)
            if near:
                near_sum[j][rows, :] = one
            else:
                joined[rows, pl.ds(768 * j, 768)] = (near_sum[j][rows, :] + one).astype(BF)

    for j in range(3):
        finish_near(j)
    project(0, True)
    second(0)
    turn(ctx, cot)
    for i in range(4):
        ugate[i] = one_row(units[6 * i : 6 * i + 6, :].astype(F32))
    vec[0:1, :] = head_lanes(heads)
    vec[1:2, :] = one_row(hidden[...].astype(F32))
    vec[2:3, :] = one_row(gain_in[...])
    vec[3:4, :] = one_row(bias_in[...])
    hgate, mgate, gain, bias = (vec.at[i : i + 1] for i in range(4))
    project(1, True)
    second(1)
    project(2, True)
    third(0)
    backs(0, 2)
    second(2)
    for j in range(3, NPIECE):
        first(j)
    tokT[...] = tokens[...].T
    tok_copy = pltpu.make_async_copy(tokT, o_tokT, out_sem.at[0])
    tok_copy.start()
    third(1)
    backs(2, 4)
    finish_far(0)
    project(0, False)
    third(2)
    finish_far(1)
    project(1, False)
    finish_far(2)
    wq_copy = pltpu.make_async_copy(wq, o_wq, out_sem.at[1])
    wq_copy.start()
    project(2, False)
    joined_copy = pltpu.make_async_copy(joined, o_joined, out_sem.at[2])
    joined_copy.start()

    scale = LOG2E / math.sqrt(HD)
    half_iota = lax.broadcasted_iota(jnp.int32, (1, 128), 1) // HD
    halves = [(half_iota == e).astype(F32).astype(BF) for e in range(2)]

    def by_head(v):
        return jnp.concatenate([v * halves[0], v * halves[1]], axis=0)

    def attend(i):
        b = i // 6
        p = i % 6
        lane = pl.multiple_of(p * 128, 128)
        for part in range(2):
            rows = pl.ds(pl.multiple_of(b * BLK + part * HALF, HALF), HALF)
            q = joined[rows, pl.ds(lane, 128)]
            k = joined[rows, pl.ds(D + lane, 128)]
            v = joined[rows, pl.ds(2 * D + lane, 128)]
            s = nt(by_head(k), q).reshape(2, HALF, HALF) * scale
            if part:
                s = jnp.where(segcol[b] == segrow[b], s, MASKED)
            top = jnp.max(s, axis=1, keepdims=True)
            pr = jnp.exp2(s - top)
            tot = jnp.sum(pr, axis=1, keepdims=True)
            low = (pr * (1.0 / tot)).astype(BF).reshape(BLK, HALF)
            lse[pl.ds(2 * i, 2), :, part * HALF : part * HALF + HALF] = top + jnp.log(tot) * LOG2E
            total = nn(by_head(v).T, low)
            ctxT[pl.ds(lane, 128), rows] = total.astype(BF)
            ctx[rows, pl.ds(lane, 128)] = total.T.astype(BF)

    plan = {
        0: [lambda: second(3)],
        5: [lambda: second(4), lambda: third(3)],
    }

    @pl.loop(0, 12)
    def _(i):
        attend(i)
        for at_step, todo in plan.items():

            @pl.when(i == at_step)
            def _(todo=todo):
                for f in todo:
                    f()

    ctx_copy = pltpu.make_async_copy(ctx, o_ctx, out_sem.at[3])
    ctx_copy.start()
    ctxT_copy = pltpu.make_async_copy(ctxT, o_ctxT, out_sem.at[4])
    ctxT_copy.start()
    finish_near(3)
    finish_far(3)
    wo_copy = pltpu.make_async_copy(wo, o_wo, out_sem.at[5])
    wo_copy.start()

    joined_copy.wait()
    tok_copy.wait()
    ctx_copy.wait()

    @pl.loop(0, 4)
    def _(r):
        rows = pl.ds(pl.multiple_of(r * 256, 256), 256)
        gated = ctx[rows, :] * hgate[...].astype(BF)
        a = nn(gated, wo[...].reshape(D, D))
        attn[rows, :] = a
        normed, _ = row_norm(tokens[rows, :].astype(F32) + g0 * a)
        low = ((normed * gain[...] + bias[...]) * mgate[...]).astype(BF)
        hlow[rows, :] = low
        hT[:, rows] = low.T

    small[...] = jnp.zeros_like(small)

    def feed(f, between={}):
        u = 2 * ((y + f // 2) % 2) + f % 2
        begin = f == 0
        w_up = wu.at[u]
        w_down = wd.at[u]

        @pl.loop(0, 2)
        def _(r):
            rows = pl.ds(pl.multiple_of(r * 512, 512), 512)
            pre = nn(hlow[rows, :], w_up[...])
            back = nn(blow[rows, :], w_down[...])
            active, slope = gelu_parts(pre)
            gate = ugate[u]
            small[pl.ds(u, 1), :] += colsum(back * active)
            a_low = (active * gate).astype(BF)
            i_low = (back * gate * slope).astype(BF)
            act[rows, :] = a_low
            inner[rows, :] = i_low
            up_part = nt(a_low, w_down[...])
            back_part = nt(i_low, w_up[...])
            if begin:
                branch[rows, :] = up_part
                hback[rows, :] = back_part
            else:
                branch[rows, :] += up_part
                hback[rows, :] += back_part
            for at_row, todo in between.items():
                pl.when(r == at_row)(todo)

        for which, (left, right) in enumerate(((hT, inner), (bT, act))):

            @pl.loop(0, 2)
            def _(r, which=which, left=left, right=right):
                rr = pl.ds(pl.multiple_of(r * SB, 128), SB)
                g = nn(left[rr, :], right[...]).astype(BF)
                for j in range(2):
                    grads[f, 4 * which + 2 * r + j] = g[:, SB * j : SB * j + SB].reshape(
                        2, 2, 2, 48, SB
                    )

    def swap1(f):
        return pltpu.make_async_remote_copy(
            src_ref=grads.at[f, :, 1 - c],
            dst_ref=got1.at[f],
            send_sem=c_send.at[f],
            recv_sem=c_recv.at[f],
            device_id=sib,
            device_id_type=MESH,
        )

    def swap2(f):
        return pltpu.make_async_remote_copy(
            src_ref=grads.at[f, pl.ds(0, MOVED[f]), c, :, 1 - x],
            dst_ref=got2.at[f, pl.ds(0, MOVED[f])],
            send_sem=x_send.at[f],
            recv_sem=x_recv.at[f],
            device_id=xpeer,
            device_id_type=MESH,
        )

    def plus(left, right):
        return (left.astype(F32) + right.astype(F32)).astype(BF)

    def sum1(f):
        swap1(f).wait_recv()

        @pl.loop(0, 8)
        def _(i):
            grads[f, i, c] = plus(grads[f, i, c], got1[f, i])

    for j in range(4, NPIECE):
        finish_near(j)

    def spread(f):
        sum1(f)
        swap2(f).start()

    def finish(f):
        swap2(f).wait_recv()

        @pl.loop(0, MOVED[f])
        def _(i):
            for yy in range(2):
                grads[f, i, c, yy, x] = plus(grads[f, i, c, yy, x], got2[f, i, yy])

        sums_copy(f).start()

    def sums_copy(f):
        return pltpu.make_async_copy(
            grads.at[f, pl.ds(0, MOVED[f]), c, :, x],
            o_sums.at[f, pl.ds(0, MOVED[f])],
            out_sem.at[9 + f],
        )

    def in_turn(*steps):
        def run():
            for step, i in steps:
                step(i)

        return run

    feed(0, {0: in_turn((second, 5), (third, 4)), 1: in_turn((second, 6))})
    swap1(0).start()
    feed(1, {0: in_turn((second, 7), (third, 5), (spread, 0)), 1: in_turn((third, 6))})
    swap1(1).start()
    third(7)
    for j in range(4, NPIECE):
        finish_far(j)
    feed(2, {0: in_turn((spread, 1))})
    swap1(2).start()
    feed(3, {0: in_turn((spread, 2)), 1: in_turn((finish, 0))})
    swap1(3).start()

    lane = lax.broadcasted_iota(jnp.int32, (1, D), 1)

    @pl.loop(0, 4)
    def _(r):
        rows = pl.ds(pl.multiple_of(r * 256, 256), 256)
        a = attn[rows, :]
        normed, inv = row_norm(tokens[rows, :].astype(F32) + g0 * a)
        plain = normed * gain[...] + bias[...]
        back = cot[rows, :].astype(F32)
        br = branch[rows, :]
        outv[rows, :] = (plain * mgate[...] + g1 * br).astype(BF)
        total = back + hback[rows, :]
        masked = total * mgate[...]
        small[4:5, :] += colsum(masked * normed)
        small[5:6, :] += colsum(masked)
        small[6:7, :] += colsum(total * plain)
        n = masked * gain[...]
        grad = (
            n
            - jnp.mean(n, axis=-1, keepdims=True)
            - normed * jnp.mean(n * normed, axis=-1, keepdims=True)
        ) * inv
        hback[rows, :] = grad
        small[7:8, :] += colsum(grad * a)
        small[8:9, :] += colsum(back * br)

    out_copy = pltpu.make_async_copy(outv, o_out, out_sem.at[6])
    out_copy.start()
    sgrad_copy = pltpu.make_async_copy(hback, o_sgrad, out_sem.at[7])
    sgrad_copy.start()
    sum1(3)
    grad_copies = [
        pltpu.make_async_copy(
            grads.at[2, pl.ds(MOVED[2], LEFT), c], o_far.at[pl.ds(0, LEFT)], out_sem.at[8]
        ),
        pltpu.make_async_copy(grads.at[3, :, c], o_far.at[pl.ds(LEFT, 8)], out_sem.at[12]),
    ]
    for copy in grad_copies:
        copy.start()
    finish(1)
    finish(2)
    for f in range(3):
        sums_copy(f).wait()
    for copy in grad_copies:
        copy.wait()
    for copy in (wq_copy, ctxT_copy, wo_copy, out_copy, sgrad_copy):
        copy.wait()
    for f in range(4):
        swap1(f).wait_send()
    for f in range(3):
        swap2(f).wait_send()
    for j in range(NPIECE):
        finish_sends(j)


def run_forward(*arrays):
    sds = jax.ShapeDtypeStruct
    outs = (
        sds((ROWS, D), BF),
        sds((ROWS, 3 * D), BF),
        sds((ROWS, D), BF),
        sds((D, ROWS), BF),
        sds((D, ROWS), BF),
        sds((ROWS, D), F32),
        sds((3, 8, 2, 48, SB), BF),
        sds((LEFT + 8, 2, 2, 48, SB), BF),
        sds((4, 192, 3 * D), BF),
        sds((4, 192, D), BF),
        sds((24, 1, BLK), F32),
        sds((16, D), F32),
    )
    any_ = pl.BlockSpec(memory_space=pl.ANY)
    vm = pl.BlockSpec(memory_space=pltpu.VMEM)
    sm = pl.BlockSpec(memory_space=pltpu.SMEM)
    return pl.pallas_call(
        forward_kernel,
        out_shape=outs,
        in_specs=[sm] * 2 + [any_] * 2 + [vm] * 5 + [any_] * 4,
        out_specs=[any_] * 10 + [vm] * 2,
        scratch_shapes=[
            pltpu.VMEM((4, 192, 3 * D), BF),
            pltpu.VMEM((4, 192, D), BF),
            pltpu.VMEM((4, D, D), BF),
            pltpu.VMEM((4, D, D), BF),
            pltpu.VMEM((ROWS, 3 * D), BF),
            pltpu.VMEM((ROWS, D), BF),
            pltpu.VMEM((D, ROWS), BF),
            pltpu.VMEM((D, ROWS), BF),
            pltpu.VMEM((ROWS, D), F32),
            pltpu.VMEM((ROWS, D), BF),
            pltpu.VMEM((D, ROWS), BF),
            pltpu.VMEM((ROWS, D), F32),
            pltpu.VMEM((ROWS, D), F32),
            pltpu.VMEM((4, 8, 2, 2, 2, 48, SB), BF),
            pltpu.VMEM((4, 8, 2, 2, 48, SB), BF),
            pltpu.VMEM((3, 8, 2, 48, SB), BF),
            pltpu.VMEM((ROWS, D), BF),
            pltpu.VMEM((ROWS, D), BF),
            pltpu.VMEM((2, HALF, 1), F32),
            pltpu.VMEM((2, 1, HALF), F32),
            pltpu.VMEM((4, 1, D), F32),
            pltpu.VMEM((8, D), F32),
            pltpu.SemaphoreType.DMA((NPIECE, 5)),
            pltpu.SemaphoreType.DMA((NPIECE, 5)),
            pltpu.SemaphoreType.DMA((NPIECE,)),
            pltpu.SemaphoreType.DMA((13,)),
            pltpu.SemaphoreType.DMA((4,)),
            pltpu.SemaphoreType.DMA((4,)),
            pltpu.SemaphoreType.DMA((3,)),
            pltpu.SemaphoreType.DMA((3,)),
        ],
        compiler_params=pltpu.CompilerParams(
            collective_id=1, has_side_effects=True, vmem_limit_bytes=64 << 20
        ),
    )(*arrays)


SENT = (12, 13, 14, 15, 0, 2, 4, 6, 8, 10, 1, 3, 5, 7, 9, 11)
GROUPS = (None,) * 4 + ((32, 4, 2), (36, 6, 3), (42, 6, 3))
FF_BLOCKS = 32
PARTS = 3
PER = 6 // PARTS


def backward_kernel(
    gates,
    heads,
    order,
    small_in,
    segs,
    lse,
    sums_in,
    far_in,
    joined_in,
    ctx_in,
    ctxT_in,
    tokT_in,
    sgrad_in,
    wq_in,
    wo_in,
    out_in,
    o_out,
    o_igrad,
    o_full,
    small_out,
    joined,
    ctx,
    ctxT,
    tokT,
    sgrad,
    wq,
    wo,
    outb,
    cgrad,
    igrad,
    ownv,
    farv,
    gotx,
    goty,
    ga,
    got1,
    got2,
    got3,
    part,
    gotz,
    total,
    slots,
    gz,
    gfull,
    sm_all,
    sm_rows,
    sm_lanes,
    sm_z,
    sm_back,
    sm_got1,
    sm_got2,
    sm_got3,
    segcol,
    segrow,
    hrow,
    hcol,
    load_sem,
    half_sem,
    ff_send,
    ff_recv,
    send_sem,
    recv_sem,
    z_send,
    z_recv,
    a_send,
    a_recv,
    f_send,
    f_recv,
    s_send,
    s_recv,
    out_sem,
):
    z, x, y, c = coords()
    g0 = gates[0]
    sib = at(z, x, y, 1 - c)
    ypeer = at(z, x, 1 - y, c)
    xpeer = at(z, 1 - x, y, c)
    diag = at(z, 1 - x, 1 - y, c)
    zpeers = [at((z + k) % 4, x, y, c) for k in (1, 2, 3)]

    loads = [
        pltpu.make_async_copy(src, dst, load_sem.at[i])
        for i, (src, dst) in enumerate(
            (
                (sgrad_in, sgrad),
                (wo_in, wo),
                (ctx_in, ctx),
                (ctxT_in, ctxT),
                (joined_in, joined),
                (tokT_in, tokT),
                (wq_in, wq),
                (out_in, ctx),
            )
        )
    ]
    halves_in = [
        pltpu.make_async_copy(sums_in.at[pl.ds(0, 2), :, y], ownv.at[pl.ds(0, 2)], half_sem.at[0]),
        pltpu.make_async_copy(far_in.at[:, :, x], farv, half_sem.at[1]),
        pltpu.make_async_copy(
            sums_in.at[2, pl.ds(0, MOVED[2]), y], ownv.at[2, pl.ds(0, MOVED[2])], half_sem.at[2]
        ),
    ]
    for copy in loads[:4]:
        copy.start()

    barrier = pltpu.get_barrier_semaphore()
    for peer in [sib, ypeer, xpeer, diag] + zpeers:
        pl.semaphore_signal(barrier, inc=1, device_id=peer, device_id_type=MESH)
    pl.semaphore_wait(barrier, 7)

    def remote(src, dst, sems, dev):
        return pltpu.make_async_remote_copy(
            src_ref=src,
            dst_ref=dst,
            send_sem=sems[0],
            recv_sem=sems[1],
            device_id=dev,
            device_id_type=MESH,
        )

    def pair(g, k):
        return send_sem.at[g, k], recv_sem.at[g, k]

    def first_block(f):
        return 8 * (2 * ((y + f // 2) % 2) + f % 2)

    def span(g):
        return (first_block(g), 8) if g < 4 else GROUPS[g][:2]

    def over_y(i):
        src, to = (
            (lambda: sums_in.at[0, :, 1 - y], goty.at[2]),
            (lambda: sums_in.at[1, :, 1 - y], goty.at[3]),
            (lambda: sums_in.at[2, pl.ds(0, MOVED[2]), 1 - y], goty.at[0, pl.ds(0, MOVED[2])]),
            (lambda: farv.at[pl.ds(0, LEFT), 1 - y], goty.at[0, pl.ds(MOVED[2], LEFT)]),
            (lambda: farv.at[pl.ds(LEFT, 8), 1 - y], goty.at[1]),
        )[i]
        return remote(src(), to, (ff_send.at[i], ff_recv.at[i]), ypeer)

    def over_x(i):
        part = (pl.ds(0, LEFT), pl.ds(LEFT, 8))[i]
        return remote(
            far_in.at[part, :, 1 - x], gotx.at[part], (ff_send.at[5 + i], ff_recv.at[5 + i]), xpeer
        )

    def mine(g, first, count):
        return ga.at[pl.ds(GROUPS[g][0] + first - FF_BLOCKS, count), c]

    def swap1(g):
        base, count, _ = GROUPS[g]
        src = ga.at[pl.ds(base - FF_BLOCKS, count), 1 - c]
        return remote(src, got1.at[pl.ds(base - FF_BLOCKS, count)], pair(g, 0), sib)

    def swap2(g):
        base, count, n = GROUPS[g]
        rest = count - n
        to = base - FF_BLOCKS
        found = [
            remote(mine(g, n, rest).at[:, :, 1 - x], got2.at[pl.ds(to + n, rest)], pair(g, 2), xpeer)
        ]
        if n:
            found.append(remote(mine(g, 0, n).at[:, 1 - y], got2.at[pl.ds(to, n)], pair(g, 1), ypeer))
        return found

    def swap3(g):
        base, count, n = GROUPS[g]
        rest = count - n
        to = base - FF_BLOCKS
        found = [
            remote(mine(g, n, rest).at[:, 1 - y, x], got3.at[pl.ds(to + n, rest)], pair(g, 4), ypeer)
        ]
        if n:
            found.append(remote(mine(g, 0, n).at[:, y, 1 - x], got3.at[pl.ds(to, n)], pair(g, 3), xpeer))
        return found

    def plus(left, right):
        return (left.astype(F32) + right.astype(F32)).astype(BF)

    def step1(g):
        base, count, _ = GROUPS[g]
        swap1(g).wait_recv()

        @pl.loop(base - FF_BLOCKS, base - FF_BLOCKS + count)
        def _(i):
            ga[i, c] = plus(ga[i, c], got1[i])

        for copy in swap2(g):
            copy.start()

    def step2(g):
        base, count, n = GROUPS[g]
        for copy in swap2(g):
            copy.wait_recv()

        @pl.loop(base - FF_BLOCKS, base - FF_BLOCKS + n)
        def _(i):
            ga[i, c, y] = plus(ga[i, c, y], got2[i])

        @pl.loop(base - FF_BLOCKS + n, base - FF_BLOCKS + count)
        def _(i):
            for yy in range(2):
                ga[i, c, yy, x] = plus(ga[i, c, yy, x], got2[i, yy])

        for copy in swap3(g):
            copy.start()

    def feed_far(n):
        over_x(n).wait_recv()

        @pl.loop(*((0, LEFT), (LEFT, LEFT + 8))[n])
        def _(i):
            farv[i] = plus(farv[i], gotx[i])

        over_y(3 + n).start()

    spare = 1 + c

    def unit(zz):
        return zz - (zz + 3 - spare) // 4

    def swapz(g, k):
        base, count = span(g)
        return remote(
            part.at[pl.ds(base, count), unit((z + k) % 4)],
            gotz.at[k - 1, pl.ds(base, count)],
            (z_send.at[g, k - 1], z_recv.at[g, k - 1]),
            zpeers[k - 1],
        )

    def step3(g):
        base, count = span(g)
        if g < 4:
            for i in ((2, 3), (4,), (0,), (1,))[g]:
                over_y(i).wait_recv()
        else:
            for copy in swap3(g):
                copy.wait_recv()
        moved = (8, 8, MOVED[2], 0)[g] if g < 4 else 0

        if moved:

            @pl.loop(0, moved)
            def _(i):
                part[base + i] = plus(ownv[g, i], goty[g, i]).reshape(3, 16, SB)

        @pl.loop(moved, count)
        def _(i):
            if g < 4:
                value = plus(farv[i - (8 - LEFT) if g == 2 else LEFT + i, y], goty[g, i])
            else:
                value = plus(ga[base - FF_BLOCKS + i, c, y, x], got3[base - FF_BLOCKS + i])
            part[base + i] = value.reshape(3, 16, SB)

        for k in (1, 2, 3):

            @pl.when((z + k) % 4 != spare)
            def _(k=k):
                swapz(g, k).start()

    def step4(g):
        base, count = span(g)

        @pl.when(z != spare)
        def _():
            for k in (1, 2, 3):
                swapz(g, k).wait_recv()

            @pl.loop(0, count)
            def _(i):
                value = part[base + i, unit(z)].astype(F32)
                for k in range(3):
                    value = value + gotz[k, base + i].astype(F32)
                total[base + i] = value.astype(BF)

    def small_copy(k):
        rows = pl.ds(pl.multiple_of(8 * c, 8), 8)
        away = pl.ds(pl.multiple_of(8 * (1 - c), 8), 8)
        lanes = pl.ds(pl.multiple_of(SB * y, 128), SB)
        other = pl.ds(pl.multiple_of(SB * (1 - y), 128), SB)
        src, dst, dev = (
            (sm_all.at[away], sm_got1, sib),
            (sm_rows.at[:, other], sm_got2, ypeer),
            (sm_lanes, sm_got3, xpeer),
            (sm_z.at[z], sm_z.at[z], zpeers[0]),
            (sm_z.at[z], sm_z.at[z], zpeers[1]),
            (sm_z.at[z], sm_z.at[z], zpeers[2]),
            (sm_back.at[rows, lanes], sm_back.at[rows, lanes], ypeer),
            (sm_back.at[rows], sm_back.at[rows], sib),
        )[k]
        return remote(src, dst, (s_send.at[k], s_recv.at[k]), dev)

    def small_take(stage):
        rows = pl.ds(pl.multiple_of(8 * c, 8), 8)
        away = pl.ds(pl.multiple_of(8 * (1 - c), 8), 8)
        lanes = pl.ds(pl.multiple_of(SB * y, 128), SB)
        other = pl.ds(pl.multiple_of(SB * (1 - y), 128), SB)
        if stage == 0:
            small_copy(0).wait_recv()
            sm_rows[...] = sm_all[rows, :] + sm_got1[...]
            small_copy(1).start()
        elif stage == 1:
            small_copy(1).wait_recv()
            sm_lanes[...] = sm_rows[:, lanes] + sm_got2[...]
            small_copy(2).start()
        elif stage == 2:
            small_copy(2).wait_recv()
            sm_z[z] = sm_lanes[...] + sm_got3[...]
            for k in (3, 4, 5):
                small_copy(k).start()
        elif stage == 3:
            for k in (1, 2, 3):
                sender = (z + 4 - k) % 4
                remote(
                    sm_z.at[sender], sm_z.at[sender], (s_send.at[2 + k], s_recv.at[2 + k]), zpeers[k - 1]
                ).wait_recv()
            sm_back[rows, lanes] = sm_z[0] + sm_z[1] + sm_z[2] + sm_z[3]
            small_copy(6).start()
        elif stage == 4:
            remote(
                sm_back.at[rows, other], sm_back.at[rows, other], (s_send.at[6], s_recv.at[6]), ypeer
            ).wait_recv()
            small_copy(7).start()
        else:
            remote(sm_back.at[away], sm_back.at[away], (s_send.at[7], s_recv.at[7]), sib).wait_recv()
            small_out[...] = sm_back[...]

    for n in range(2):
        over_x(n).start()
    for i in range(3):
        over_y(i).start()
    for copy in [loads[4]] + halves_in + loads[5:7]:
        copy.start()

    begin = first_rows(segs)
    turn_labels(segs, begin, segcol, segrow)
    hrow[...] = head_lanes(heads)
    hcol[...] = jnp.broadcast_to(hrow[...], (8, D)).T[:, 0:1]
    hgate = hrow
    sm_all[...] = small_in[...]
    loads[0].wait()
    loads[1].wait()
    loads[2].wait()

    @pl.loop(0, 4)
    def _(r):
        rows = pl.ds(pl.multiple_of(r * 256, 256), 256)
        low = (g0 * sgrad[rows, :]).astype(BF)
        outb[rows, :] = low
        grad = nt(low, wo[...].reshape(D, D)).astype(BF)
        sm_all[9:10, :] += colsum(ctx[rows, :].astype(F32) * grad.astype(F32))
        cgrad[rows, :] = grad * hgate[...].astype(BF)

    small_copy(0).start()
    loads[7].start()
    loads[3].wait()

    def weight_tiles(left, right, lane, rowgate, places):
        @pl.loop(0, 2)
        def _(r):
            rr = pl.ds(pl.multiple_of(r * SB, 128), SB)
            g = nn(left[rr, :], right[:, pl.ds(lane, SB)])
            if rowgate is not None:
                g = g * rowgate[rr, :]
            ga[places[0] + r * (places[1] - places[0])] = g.astype(BF).reshape(2, 2, 2, 48, SB)

    for j in range(2):
        weight_tiles(ctxT, outb, SB * j, hcol, (SENT.index(12 + j), SENT.index(14 + j)))

    swap1(4).start()
    loads[4].wait()

    scale = LOG2E / math.sqrt(HD)
    factor = 1.0 / math.sqrt(HD)
    half_iota = lax.broadcasted_iota(jnp.int32, (1, 128), 1) // HD
    halves = [(half_iota == e).astype(F32).astype(BF) for e in range(2)]

    def by_head(v):
        return jnp.concatenate([v * halves[0], v * halves[1]], axis=0)

    def of_head(v):
        return jnp.where(half_iota == 0, v[:HALF], v[HALF:])

    def attend_back(i):
        p = i // 2
        b = i % 2
        lane = pl.multiple_of(p * 128, 128)
        for part in range(2):
            rows = pl.ds(pl.multiple_of(b * BLK + part * HALF, HALF), HALF)
            q = joined[rows, pl.ds(lane, 128)]
            k = joined[rows, pl.ds(D + lane, 128)]
            v = joined[rows, pl.ds(2 * D + lane, 128)]
            do = cgrad[rows, pl.ds(lane, 128)]
            k2 = by_head(k)
            s = nt(k2, q).reshape(2, HALF, HALF) * scale
            if part:
                s = jnp.where(segcol[b] == segrow[b], s, MASKED)
            first = 2 * (b * 6 + p)
            pr = jnp.exp2(s - lse[pl.ds(first, 2), :, part * HALF : part * HALF + HALF])
            dp = nt(by_head(v), do).reshape(2, HALF, HALF)
            delta = jnp.sum(pr * dp, axis=1, keepdims=True)
            ds = (pr * (dp - delta)).astype(BF).reshape(BLK, HALF)
            dqT = nn(k2.T, ds)
            dk = of_head(nn(ds, q))
            dv = of_head(nn(pr.astype(BF).reshape(BLK, HALF), do))
            joined[rows, pl.ds(lane, 128)] = (dqT * factor).T.astype(BF)
            joined[rows, pl.ds(D + lane, 128)] = (dk * factor).astype(BF)
            joined[rows, pl.ds(2 * D + lane, 128)] = dv.astype(BF)

    def qkv_tiles(h):
        for j in (h, 2 + h, 4 + h):
            weight_tiles(tokT, joined, SB * j, None, (SENT.index(j), SENT.index(6 + j)))

    def middle():
        loads[5].wait()
        qkv_tiles(0)
        swap1(5).start()

    def first_sums():
        halves_in[0].wait()
        halves_in[2].wait()
        halves_in[1].wait()
        feed_far(0)
        step3(2)

    plan = {
        0: [lambda: small_take(0)],
        1: [lambda: step1(4), first_sums],
        5: [middle],
        6: [lambda: step1(5), lambda: small_take(1)],
        7: [lambda: feed_far(1), lambda: step3(3)],
        9: [lambda: step3(0)],
        11: [lambda: step2(4)],
    }

    @pl.loop(0, 12)
    def _(i):
        attend_back(i)
        for at_step, todo in plan.items():

            @pl.when(i == at_step)
            def _(todo=todo):
                for f in todo:
                    f()

    qkv_tiles(1)
    swap1(6).start()
    loads[6].wait()

    def input_rows(lo, hi):
        @pl.loop(lo, hi)
        def _(r):
            rows = pl.ds(pl.multiple_of(r * 512, 512), 512)
            igrad[rows, :] = sgrad[rows, :] + nt(joined[rows, :], wq[...].reshape(D, 3 * D))

    step3(1)
    step1(6)
    small_take(2)
    input_rows(0, 1)
    step4(2)
    step3(4)
    step2(5)
    step4(3)
    input_rows(1, 2)
    def turn_back():
        loads[7].wait()

        @pl.loop(0, 6)
        def _(t):
            b = t // 3
            hot = turning(jnp.where(b == 0, begin[0:1], begin[1:2]), -1).astype(BF)
            rows = pl.ds(pl.multiple_of(b * BLK, BLK), BLK)
            cols = pl.ds(pl.multiple_of(t % 3 * 256, 256), 256)
            cgrad[rows, cols] = nn(hot, ctx[rows, cols]).astype(BF)
            rest = igrad[rows, cols]
            value = None
            for _ in range(3):
                high = rest.astype(BF)
                rest = rest - high.astype(F32)
                one = nn(hot, high)
                value = one if value is None else value + one
            igrad[rows, cols] = value

    step2(6)
    step3(5)
    turn_back()
    igrad_copy = pltpu.make_async_copy(igrad, o_igrad, out_sem.at[0])
    igrad_copy.start()
    out_copy = pltpu.make_async_copy(cgrad, o_out, out_sem.at[1])
    out_copy.start()
    step4(0)
    step3(6)
    step4(1)
    step4(4)
    small_take(3)
    step4(5)
    step4(6)

    def deal(n, k, to, u):
        return remote(
            slots.at[to, :, n],
            gz.at[:, n, :, u],
            (a_send.at[n, k - 1], a_recv.at[n, k - 1]),
            zpeers[k - 1],
        )

    @pl.when(z != spare)
    def _():
        @pl.loop(0, 48)
        def _(s):
            slots[s // 12, s // 6 % 2, s // PER % PARTS, s % PER] = total[order[s]]

        for n in range(PARTS):
            for k in (1, 2, 3):
                deal(n, k, (z + k) % 4, unit(z)).start()
            gz[:, n, :, unit(z)] = slots[z, :, n]

    def piece(n, cc, yy, xx):
        return gfull.at[n, :, 4 * cc + 2 * yy + xx]

    others = ((y, 1 - x), (1 - y, x), (1 - y, 1 - x))

    def near(n, k):
        src = gz.at[1 - x if k in (0, 2) else x, n]
        sems = (f_send.at[n, k], f_recv.at[n, k])
        return remote(src, piece(n, c, y, x), sems, (xpeer, ypeer, diag, sib)[k])

    def onward(n, k):
        yy, xx = others[k]
        to = piece(n, c, yy, xx)
        return remote(to, to, (f_send.at[n, 4 + k], f_recv.at[n, 4 + k]), sib)

    def pass_on(n):
        for k in range(3):
            near(n, k).wait_recv()
            onward(n, k).start()

    for n in range(PARTS):
        for k in (1, 2, 3):
            sender = (z + 4 - k) % 4

            @pl.when(sender != spare)
            def _(n=n, k=k, sender=sender):
                deal(n, k, z, unit(sender)).wait_recv()

        for k in range(4):
            near(n, k).start()
        gfull[n, :, 4 * c + 2 * y + x] = gz[x, n]
        if n:
            pass_on(n - 1)
    small_take(4)
    pass_on(PARTS - 1)
    small_take(5)
    for n in range(PARTS):
        near(n, 3).wait_recv()
        for k in range(3):
            onward(n, k).wait_recv()
    full_copy = pltpu.make_async_copy(gfull, o_full, out_sem.at[2])
    full_copy.start()
    for n in range(PARTS):
        for k in range(4):
            near(n, k).wait_send()
        for k in range(3):
            onward(n, k).wait_send()

        @pl.when(z != spare)
        def _(n=n):
            for k in (1, 2, 3):
                deal(n, k, (z + k) % 4, unit(z)).wait_send()

    for g in range(len(GROUPS)):
        for k in (1, 2, 3):

            @pl.when((z + k) % 4 != spare)
            def _(g=g, k=k):
                swapz(g, k).wait_send()

    for k in range(8):
        small_copy(k).wait_send()
    for g in range(4, len(GROUPS)):
        for copy in [swap1(g)] + swap2(g) + swap3(g):
            copy.wait_send()
    for i in range(5):
        over_y(i).wait_send()
    for n in range(2):
        over_x(n).wait_send()
    igrad_copy.wait()
    out_copy.wait()
    full_copy.wait()


def run_backward(*arrays):
    sds = jax.ShapeDtypeStruct
    outs = (sds((ROWS, D), BF), sds((ROWS, D), F32), sds((PARTS, PER, 8, 3, 16, SB), BF), sds((16, D), F32))
    any_ = pl.BlockSpec(memory_space=pl.ANY)
    vm = pl.BlockSpec(memory_space=pltpu.VMEM)
    sm = pl.BlockSpec(memory_space=pltpu.SMEM)
    dma = pltpu.SemaphoreType.DMA
    return pl.pallas_call(
        backward_kernel,
        out_shape=outs,
        in_specs=[sm] * 3 + [vm] * 3 + [any_] * 10,
        out_specs=[any_] * 3 + [vm],
        scratch_shapes=[
            pltpu.VMEM((ROWS, 3 * D), BF),
            pltpu.VMEM((ROWS, D), BF),
            pltpu.VMEM((D, ROWS), BF),
            pltpu.VMEM((D, ROWS), BF),
            pltpu.VMEM((ROWS, D), F32),
            pltpu.VMEM((4, 192, 3 * D), BF),
            pltpu.VMEM((4, 192, D), BF),
            pltpu.VMEM((ROWS, D), BF),
            pltpu.VMEM((ROWS, D), BF),
            pltpu.VMEM((ROWS, D), F32),
            pltpu.VMEM((3, 8, 48, SB), BF),
            pltpu.VMEM((LEFT + 8, 2, 48, SB), BF),
            pltpu.VMEM((LEFT + 8, 2, 48, SB), BF),
            pltpu.VMEM((4, 8, 48, SB), BF),
            pltpu.VMEM((16, 2, 2, 2, 48, SB), BF),
            pltpu.VMEM((16, 2, 2, 48, SB), BF),
            pltpu.VMEM((16, 2, 48, SB), BF),
            pltpu.VMEM((16, 48, SB), BF),
            pltpu.VMEM((48, 3, 16, SB), BF),
            pltpu.VMEM((3, 48, 16, SB), BF),
            pltpu.VMEM((48, 16, SB), BF),
            pltpu.VMEM((4, 2, PARTS, PER, 16, SB), BF),
            pltpu.VMEM((2, PARTS, PER, 3, 16, SB), BF),
            pltpu.VMEM((PARTS, PER, 8, 3, 16, SB), BF),
            pltpu.VMEM((16, D), F32),
            pltpu.VMEM((8, D), F32),
            pltpu.VMEM((8, SB), F32),
            pltpu.VMEM((4, 8, SB), F32),
            pltpu.VMEM((16, D), F32),
            pltpu.VMEM((8, D), F32),
            pltpu.VMEM((8, SB), F32),
            pltpu.VMEM((8, SB), F32),
            pltpu.VMEM((2, HALF, 1), F32),
            pltpu.VMEM((2, 1, HALF), F32),
            pltpu.VMEM((1, D), F32),
            pltpu.VMEM((D, 1), F32),
            dma((8,)),
            dma((3,)),
            dma((7,)),
            dma((7,)),
            dma((7, 5)),
            dma((7, 5)),
            dma((7, 3)),
            dma((7, 3)),
            dma((PARTS, 3)),
            dma((PARTS, 3)),
            dma((PARTS, 7)),
            dma((PARTS, 7)),
            dma((8,)),
            dma((8,)),
            dma((3,)),
        ],
        compiler_params=pltpu.CompilerParams(
            collective_id=2, has_side_effects=True, vmem_limit_bytes=64 << 20
        ),
    )(*arrays)


def split(value):
    high = value.astype(BF)
    return high, (value - high.astype(F32)).astype(BF)


def update_kernel(
    small,
    gain,
    bias,
    full,
    master,
    left_stats,
    right_stats,
    left_root,
    right_root,
    out_in,
    igrad_in,
    o_grad,
    o_left,
    o_right,
    o_new,
    o_copy,
    o_unit,
    o_hidden,
    o_head,
    o_layer,
    o_norm,
    o_norm_new,
    o_out,
    o_igrad,
    turned,
    stage_out,
    stage_igrad,
    sem,
):
    slot = pl.program_id(0)
    moves_in = (
        pltpu.make_async_copy(out_in, stage_out, sem.at[0]),
        pltpu.make_async_copy(igrad_in, stage_igrad, sem.at[1]),
    )
    moves = (
        pltpu.make_async_copy(stage_out, o_out, sem.at[2]),
        pltpu.make_async_copy(stage_igrad, o_igrad, sem.at[3]),
    )

    @pl.when(slot == 0)
    def _():
        for move in moves_in:
            move.start()
        for i in range(4):
            o_unit[6 * i : 6 * i + 6, :] = many_rows(small[i : i + 1, :])
        o_hidden[...] = many_rows(small[6:7, :])
        o_norm[...] = small[4:6, :]
        rate = 0.2 / math.sqrt(ROWS * 32)
        o_norm_new[0:1, :] = one_row(gain[...]) - rate * small[4:5, :]
        o_norm_new[1:2, :] = one_row(bias[...]) - rate * small[5:6, :]
        lane = lax.broadcasted_iota(jnp.int32, (16, D), 1) // HD
        row = lax.broadcasted_iota(jnp.int32, (16, D), 0)
        by_head = jnp.sum(jnp.where(lane == row, small[9:10, :], 0.0), axis=1, keepdims=True)
        square = lax.broadcasted_iota(jnp.int32, (16, 128), 1)
        diagonal = square == lax.broadcasted_iota(jnp.int32, (16, 128), 0)
        o_head[...] = jnp.sum(jnp.where(diagonal, by_head, 0.0), axis=0, keepdims=True)[:, :12]
        pair = jnp.sum(small[7:9, :], axis=1, keepdims=True)
        first = lax.broadcasted_iota(jnp.int32, (1, 2), 1) == 0
        o_layer[...] = jnp.where(first, pair[0:1], pair[1:2])

    start = pl.multiple_of(lax.axis_index("mp") * 96, 16)
    own = full[0, pl.ds(start, 96), :]
    whole = full[0]
    o_grad[0] = own.astype(F32)
    o_left[0] = BETA * left_stats[0] + (1.0 - BETA) * nt(own, whole)
    turned[...] = whole.T
    root_high, root_low = split(left_root[0])
    stack = nn(jnp.concatenate([turned[pl.ds(start, 96), :], root_high, root_low], axis=0), whole)
    o_right[0] = BETA * right_stats[0] + (1.0 - BETA) * stack[:96]
    part_high, part_low = split(stack[96:192] + stack[192:])
    right_high, right_low = split(right_root[0])
    pair = nn(jnp.concatenate([part_high, part_low], axis=0), right_high)
    update = pair[:96] + pair[96:] + nn(part_high, right_low)
    new = master[0] - RATE * update
    o_new[0] = new
    o_copy[0] = new.astype(BF)

    @pl.when(slot == 2)
    def _():
        for first, then in zip(moves_in, moves):
            first.wait()
            then.start()

    @pl.when(slot == 5)
    def _():
        for move in moves:
            move.wait()


def run_update(*arrays):
    sds = jax.ShapeDtypeStruct
    whole = pl.BlockSpec((1, SB, SB), lambda s: (s, 0, 0))
    rows = pl.BlockSpec((1, 96, SB), lambda s: (s, 0, 0))
    any_ = pl.BlockSpec(memory_space=pl.ANY)

    def const(*shape):
        return pl.BlockSpec(shape, lambda s: (0, 0))

    flat = const(6, 128)
    return pl.pallas_call(
        update_kernel,
        grid=(6,),
        out_shape=(sds((6, 96, SB), F32),) * 4
        + (
            sds((6, 96, SB), BF),
            sds((24, 128), F32),
            sds((6, 128), F32),
            sds((1, 12), F32),
            sds((1, 2), F32),
            sds((2, D), F32),
            sds((2, D), F32),
            sds((ROWS, D), BF),
            sds((ROWS, D), F32),
        ),
        in_specs=[const(16, D), flat, flat, whole] + [rows] * 4 + [whole] + [any_] * 2,
        out_specs=[rows] * 5
        + [const(24, 128), flat, const(1, 12), const(1, 2), const(2, D), const(2, D), any_, any_],
        scratch_shapes=[
            pltpu.VMEM((SB, SB), BF),
            pltpu.VMEM((ROWS, D), BF),
            pltpu.VMEM((ROWS, D), F32),
            pltpu.SemaphoreType.DMA((4,)),
        ],
        compiler_params=pltpu.CompilerParams(vmem_limit_bytes=64 << 20),
    )(*arrays)


PLACE = tuple(FF_BLOCKS + SENT.index(b) for b in range(16)) + tuple(
    8 * (col // 2) + 4 * which + 2 * row + col % 2 for which in range(2) for row in range(2) for col in range(8)
)


def fast_body(
    tokens,
    segments,
    head_mask,
    unit_mask,
    hidden_mask,
    layer_gates,
    qkv_weight,
    out_weight,
    norm_gain,
    norm_bias,
    up_weight,
    down_weight,
    cotangent,
    owner_slot,
    master,
    left_stats,
    right_stats,
    left_root,
    right_root,
):
    gain = norm_gain.reshape(6, 128)
    bias = norm_bias.reshape(6, 128)
    (output, joined, ctx, ctxT, tokT, summed_grad, sums, far, wq, wo, lse, small) = run_forward(
        layer_gates,
        head_mask,
        tokens,
        cotangent,
        segments,
        unit_mask.reshape(24, 128),
        hidden_mask.reshape(6, 128),
        gain,
        bias,
        qkv_weight,
        out_weight,
        up_weight,
        down_weight,
    )
    slot_order = jnp.sum(
        jnp.where(owner_slot[None, :] == jnp.arange(48)[:, None], jnp.asarray(PLACE)[None, :], 0), axis=1
    )
    output, input_grad, full, small = run_backward(
        layer_gates,
        head_mask,
        slot_order,
        small,
        segments,
        lse,
        sums,
        far,
        joined,
        ctx,
        ctxT,
        tokT,
        summed_grad,
        wq,
        wo,
        output,
    )
    (
        owned,
        left_new,
        right_new,
        weight_new,
        weight_copy,
        unit_grad,
        hidden_grad,
        head_grad,
        layer_grad,
        norm_grad,
        norm_new,
        output,
        input_grad,
    ) = run_update(
        small,
        gain,
        bias,
        full.reshape(6, SB, SB),
        master,
        left_stats,
        right_stats,
        left_root,
        right_root,
        output,
        input_grad,
    )
    return (
        output,
        input_grad,
        head_grad.reshape(12),
        unit_grad.reshape(FF),
        hidden_grad.reshape(D),
        layer_grad.reshape(2),
        norm_grad,
        norm_new,
        owned,
        left_new,
        right_new,
        weight_new,
        weight_copy,
    )


def solution(mesh):
    return jax.shard_map(
        fast_body if dict(mesh.shape) == {"dp": 8, "mp": 4} else body,
        mesh=mesh,
        in_specs=(
            P(("dp", "mp"), None),
            P(("dp", "mp"), None),
            P(),
            P(),
            P(),
            P(),
            P("mp", None),
            P("mp", None),
            P(),
            P(),
            P(None, "mp"),
            P(None, "mp"),
            P(("dp", "mp"), None),
            P(),
            P("dp", "mp", None),
            P("dp", "mp", None),
            P("dp", "mp", None),
            P("dp", "mp", None),
            P("dp", None, None),
        ),
        out_specs=(
            P(("dp", "mp"), None),
            P(("dp", "mp"), None),
            P(),
            P(),
            P(),
            P(),
            P(),
            P(),
            P("dp", "mp", None),
            P("dp", "mp", None),
            P("dp", "mp", None),
            P("dp", "mp", None),
            P("dp", "mp", None),
        ),
        check_vma=False,
    )
```

profile of v0, /device:TPU:9, one launch (start us, length us, event | category | flops | bytes accessed | tf_op | source)
XLA Modules:
  0.0 188.7 jit_solution(18005400139945983088)
XLA Ops:
  0.6 1.3 select_reduce_fusion.order
  1.9 92.8 %shard_map.291 = (bf16[1024,768]{1,0:T(8,128)(2,1)}, bf16[1024,2304]{1,0:T(8,128)(2,1)}, bf16[1024,768]{1,0:T(8,128)(2,1)}, bf16[768,1024]{1,0:T(8,128)(2,1)}, b...) custom-call(f32[2]{0:T(128)} %gates.3, s32[12]{0:T(128)} %heads.3, ...), custom_call_target="tpu_custom_call" | custom-call | tf_op jit(solution)/shard_map/pallas_call | solution.py:878
  94.7 82.8 %shard_map.292 = (bf16[1024,768]{1,0:T(8,128)(2,1)}, f32[1024,768]{1,0:T(8,128)}, bf16[3,2,8,3,16,384]{5,4,3,2,1,0:T(8,128)(2,1)}, f32[16,768]{1,0:T(8,128)}) custom-call(f32[2]{0:T(128)} %gates.3, s32[12]{0:T(128)} %heads.3, s32[48]{0:T(128)} %select_reduce_fusion.order, f32[16,768]{1,0:T(8,128)} %get-tuple-element.42.small_in, s32[2,512]{1,0:T(2,128)} %segs.3, ...), custom_call_target="tpu_custom_call" | custom-call | tf_op jit(solution)/shard_map/pallas_call | solution.py:1526
  177.5 11.0 %shard_map.293 = (f32[6,96,384]{2,1,0:T(8,128)}, f32[6,96,384]{2,1,0:T(8,128)}, f32[6,96,384]{2,1,0:T(8,128)}, f32[6,96,384]{2,1,0:T(8,128)}, bf16[6,96,384]{2,1...) custom-call(f32[16,768]{1,0:T(8,128)} %get-tuple-element.54.small, ...), custom_call_target="tpu_custom_call" | custom-call | tf_op jit(solution)/shard_map/pallas_call | solution.py:1695
where the time goes:
time: 190 us; the launch traced here: 189 us
  Pallas kernels  187 us (98%)
    pallas_call x1, Pallas kernels, run_forward(): pl.pallas_call(forward_kernel, out_shape=outs, in_specs=[sm] * 2 + [any_]...  92.8 us
    pallas_call x1, Pallas kernels, run_backward(): pl.pallas_call(backward_kernel, out_shape=outs, in_specs=[sm] * 3 + [vm]...  82.8 us
    pallas_call x1, Pallas kernels, run_update(): pl.pallas_call(update_kernel, grid=(6,), out_shape=(sds((6, 96, SB), F32)...  11 us

commit v1 on v0

--- a/solution.py
+++ b/solution.py
@@ -1283,13 +1283,11 @@
     loads[3].wait()
 
     def weight_tiles(left, right, lane, rowgate, places):
-        @pl.loop(0, 2)
-        def _(r):
-            rr = pl.ds(pl.multiple_of(r * SB, 128), SB)
-            g = nn(left[rr, :], right[:, pl.ds(lane, SB)])
-            if rowgate is not None:
-                g = g * rowgate[rr, :]
-            ga[places[0] + r * (places[1] - places[0])] = g.astype(BF).reshape(2, 2, 2, 48, SB)
+        g = nn(left[...], right[:, pl.ds(lane, SB)])
+        if rowgate is not None:
+            g = g * rowgate[...]
+        for r in range(2):
+            ga[places[r]] = g[SB * r : SB * r + SB].astype(BF).reshape(2, 2, 2, 48, SB)
 
     for j in range(2):
         weight_tiles(ctxT, outb, SB * j, hcol, (SENT.index(12 + j), SENT.index(14 + j)))
@@ -1335,8 +1333,12 @@
             joined[rows, pl.ds(2 * D + lane, 128)] = dv.astype(BF)
 
     def qkv_tiles(h):
-        for j in (h, 2 + h, 4 + h):
-            weight_tiles(tokT, joined, SB * j, None, (SENT.index(j), SENT.index(6 + j)))
+        at_h = SENT.index(h)
+
+        @pl.loop(0, 3)
+        def _(j):
+            lane = pl.multiple_of(SB * (2 * j + h), 128)
+            weight_tiles(tokT, joined, lane, None, (at_h + j, at_h + 3 + j))
 
     def middle():
         loads[5].wait()

time: 190 us -> 190 us (level)
  no operation moved by 1% of the time
where the time goes in v1:
time: 190 us; the launch traced here: 189 us
  Pallas kernels  187 us (98%)
    pallas_call x1, Pallas kernels, run_forward(): pl.pallas_call(forward_kernel, out_shape=outs, in_specs=[sm] * 2 + [any_]...  92.8 us
    pallas_call x1, Pallas kernels, run_backward(): pl.pallas_call(backward_kernel, out_shape=outs, in_specs=[sm] * 3 + [vm]...  82.8 us
    pallas_call x1, Pallas kernels, run_update(): pl.pallas_call(update_kernel, grid=(6,), out_shape=(sds((6, 96, SB), F32)...  11 us

profile of v1, /device:TPU:9, one launch (start us, length us, event | category | flops | bytes accessed | tf_op | source)
XLA Modules:
  0.0 188.7 jit_solution(395225665779450803)
XLA Ops:
  0.6 1.3 select_reduce_fusion.order
  1.9 92.8 %shard_map.291 = (bf16[1024,768]{1,0:T(8,128)(2,1)}, bf16[1024,2304]{1,0:T(8,128)(2,1)}, bf16[1024,768]{1,0:T(8,128)(2,1)}, bf16[768,1024]{1,0:T(8,128)(2,1)}, b...) custom-call(f32[2]{0:T(128)} %gates.3, s32[12]{0:T(128)} %heads.3, ...), custom_call_target="tpu_custom_call" | custom-call | tf_op jit(solution)/shard_map/pallas_call | solution.py:878
  94.7 82.8 %shard_map.292 = (bf16[1024,768]{1,0:T(8,128)(2,1)}, f32[1024,768]{1,0:T(8,128)}, bf16[3,2,8,3,16,384]{5,4,3,2,1,0:T(8,128)(2,1)}, f32[16,768]{1,0:T(8,128)}) custom-call(f32[2]{0:T(128)} %gates.3, s32[12]{0:T(128)} %heads.3, s32[48]{0:T(128)} %select_reduce_fusion.order, f32[16,768]{1,0:T(8,128)} %get-tuple-element.42.small_in, s32[2,512]{1,0:T(2,128)} %segs.3, ...), custom_call_target="tpu_custom_call" | custom-call | tf_op jit(solution)/shard_map/pallas_call | solution.py:1528
  177.5 11.0 %shard_map.293 = (f32[6,96,384]{2,1,0:T(8,128)}, f32[6,96,384]{2,1,0:T(8,128)}, f32[6,96,384]{2,1,0:T(8,128)}, f32[6,96,384]{2,1,0:T(8,128)}, bf16[6,96,384]{2,1...) custom-call(f32[16,768]{1,0:T(8,128)} %get-tuple-element.54.small, ...), custom_call_target="tpu_custom_call" | custom-call | tf_op jit(solution)/shard_map/pallas_call | solution.py:1697
